TPU v7x, 32 devices: a whole 2x2x4 slice. The times are simulated.
32 devices in a mesh: blk: 8 (over y, x, core), orb: 4 (over z).
Axes of the slice: x: 2, y: 2, z: 4, core: 2. Of those that a mesh axis runs over, the one named last changes fastest.
Arguments:
- green_tiles: bfloat16 [2, 192, 256, 256], P(None, 'blk'), may hold values from -6 to 6
- screen_tiles: bfloat16 [2, 96, 256, 256], P(None, 'blk', 'orb'), may hold values from -6 to 6
- coeffs: bfloat16 [12288, 2048], P('blk', 'orb'), may hold values from -0.099609375 to 0.099609375
- tile_count: int32 [8], P('blk'), may hold values from 1 to 24, 96 in all
- send_slot: int32 [8, 8, 3], P('blk'), may hold values from 0 to 11
- recv_index: int32 [8, 24], P('blk'), may hold values from 0 to 23, as said below
- row_block: int32 [8, 24], P('blk'), may hold values from 0 to 5
- col_block: int32 [8, 24], P('blk'), may hold values from 0 to 47
Outputs:
- sigma_orbital: float32 [2048, 2, 2048], P('blk', None, 'orb')
Inputs may be any that keep to these rules, and one draw needn't show every extreme that they name: `recv_index`: for each blk index and each round r < 3, the slots r * (8) to (r + 1) * 8 - 1 name every peer once, each as peer * 3 + r. `tile_count`: the counts of all blk indices sum to 96.
All inputs are finite; a program needn't handle non-finite values. No bound on the sum of `tile_count` on one device may be relied on, other than what follows from the above.
Results may differ from a plain program's by a relative error of at most 0.0041.
Values may be sent and summed in bfloat16 or wider, within the bound.
A program may use at most 128 MiB of HBM per device.

v0:
```python
import jax
import jax.numpy as jnp
from jax import lax
from jax.sharding import PartitionSpec as P


def shards(
    green_tiles, screen_tiles, coeffs, tile_count, send_slot, recv_index, row_block, col_block
):
    width = green_tiles.shape[2]
    slot_total = green_tiles.shape[1]
    owned_blocks = coeffs.shape[0] // width
    orbital_local = coeffs.shape[1]
    outgoing = send_slot.reshape(-1)
    screen_whole = lax.all_gather(screen_tiles, "orb", axis=2, tiled=True)
    packed = jnp.take(screen_whole, outgoing, axis=1)
    arrived = lax.all_to_all(packed, "blk", split_axis=1, concat_axis=1, tiled=True)
    panel = lax.all_gather(coeffs, "blk", axis=0, tiled=True)
    panel_blocks = panel.reshape(-1, width, orbital_local)
    own_rows = lax.all_gather(coeffs, "orb", axis=1, tiled=True)
    live = (jnp.arange(slot_total, dtype=jnp.int32) < tile_count[0]).astype(jnp.float32)
    targets = row_block[0]
    group = 8

    def accumulate(totals, start):
        green_part = lax.dynamic_slice_in_dim(green_tiles, start, group, 1)
        which = lax.dynamic_slice_in_dim(recv_index[0], start, group, 0)
        screen_part = jnp.take(arrived, which, axis=1)
        sigma = (-(green_part.astype(jnp.float32) * screen_part.astype(jnp.float32))).astype(
            jnp.bfloat16
        )
        columns = lax.dynamic_slice_in_dim(col_block[0], start, group, 0)
        blocks = jnp.take(panel_blocks, columns, axis=0)
        products = jnp.einsum("tsab,sbm->satm", sigma, blocks, preferred_element_type=jnp.float32)
        group_rows = lax.dynamic_slice_in_dim(targets, start, group, 0)
        group_live = lax.dynamic_slice_in_dim(live, start, group, 0)
        for member in range(group):
            target = group_rows[member]
            current = lax.dynamic_index_in_dim(totals, target, 0, keepdims=True)
            updated = current + group_live[member] * products[member][None]
            totals = lax.dynamic_update_slice_in_dim(totals, updated, target, 0)
        return (totals, None)

    starts = jnp.arange(0, slot_total, group, dtype=jnp.int32)
    empty = jnp.zeros((owned_blocks, width, 2, orbital_local), jnp.float32)
    totals, unused = lax.scan(accumulate, empty, starts)
    folded = totals.astype(jnp.bfloat16).reshape(owned_blocks * width, 2, orbital_local)
    return lax.psum_scatter(
        jnp.einsum("kn,ktm->ntm", own_rows, folded, preferred_element_type=jnp.float32),
        "blk",
        scatter_dimension=0,
        tiled=True,
    )


def solution(mesh):
    return jax.shard_map(
        shards,
        mesh=mesh,
        in_specs=(
            P(None, "blk", None, None),
            P(None, "blk", "orb", None),
            P("blk", "orb"),
            P("blk"),
            P("blk", None, None),
            P("blk", None),
            P("blk", None),
            P("blk", None),
        ),
        out_specs=P("blk", None, "orb"),
        check_vma=False,
    )
```

profile of v0, /device:TPU:0, one launch (start us, length us, event | category | flops | bytes accessed | tf_op | source)
XLA Modules:
  0.0 496.9 jit_solution(7030310610212735367)
XLA Ops:
  9.0 66.2 %all-gather.6.cloned.1.call-done = bf16[2,12,256,256]{3,2,1,0:T(8,128)(2,1)} async-done(((bf16[2,12,64,256]{3,2,1,0:T(8,128)(2,1)}), bf16[2,12,256,256]{3,2,1,0:T(8,128)(2,1)}) %all-gather.6.cloned.1.call-update) | async-done | bytes 3145744 | tf_op jit(solution)/shard_map/all_gather | solution.py:15
  75.1 6.3 %gather_fusion.2 = bf16[24,2,256,256]{3,2,1,0:T(8,128)(2,1)} fusion(bf16[2,12,256,256]{3,2,1,0:T(8,128)(2,1)} %all-gather.6.cloned.1.call-done, s32[1024]{0:T(1024)S(1)} %pad_clamp_fusion.2), kind=kCustom, calls=%fused_computation.2 | custom fusion | bytes 12583008 | tf_op jit(solution)/shard_map/jit(_take)/gather | solution.py:16
  81.4 7.0 %select_bitcast_fusion = bf16[2,24,256,256]{3,2,0,1:T(8,128)(2,1)} fusion(bf16[24,2,256,256]{3,2,1,0:T(8,128)(2,1)} %gather_fusion.2, pred[24]{0:T(512)(128)(4,1)S(1)} %compare_and_fusion.2), kind=kLoop, calls=%fused_computation.55 | loop fusion | flops 3145728 | bytes 12582936 | tf_op jit(solution)/shard_map/jit(_take)/select_n | solution.py:16
  88.4 4.8 all-to-all-start
  94.7 108.7 %all-to-all-done = bf16[2,24,256,256]{3,2,0,1:T(8,128)(2,1)} async-done(((bf16[2,24,256,256]{3,2,0,1:T(8,128)(2,1)}), bf16[2,24,256,256]{3,2,0,1:T(8,128)(2,1)}, u32[]{:S(2)}, u32[]{:S(2)}) %all-to-all-start) | async-done | bytes 6291488 | tf_op jit(solution)/shard_map/all_to_all | solution.py:17
  203.4 6.1 %copy.18 = bf16[2,24,256,256]{3,2,1,0:T(8,128)(2,1)} copy(bf16[2,24,256,256]{3,2,0,1:T(8,128)(2,1)} %all-to-all-done) | data formatting | bytes 12582912 | tf_op jit(solution)/shard_map/while | solution.py:46
  212.8 189.6 %while.10 = (s32[]{:T(128)}, f32[6,256,2,512]{1,3,2,0:T(8,128)}, s32[3]{0:T(128)S(1)}, s32[24]{0:T(128)S(1)}, f32[24]{0:T(128)S(1)}, /*index=5*/s32[1,24]{1,0:T(...) while((s32[]{:T(128)}, f32[6,256,2,512]{1,3,2,0:T(8,128)}, ...), condition=%wide.region_1.2_spmd, body=%wide.region_0.1_spmd.sunk | while | flops 1085278336 | bytes 48247880 | solution.py:46
  215.6 4.2 gather_fusion
  219.8 6.9 %gather_fusion.1 = bf16[8,256,512]{2,1,0:T(8,128)(2,1)} fusion(bf16[48,256,512]{2,1,0:T(8,128)(2,1)} %get-tuple-element.253, s32[1024]{0:T(1024)S(1)} %pad_clamp_fusion.6), kind=kCustom, calls=%fused_computation.clone.1 | custom fusion | bytes 4194336 | tf_op jit(solution)/shard_map/while/body/eval_jaxpr/jit(_take)/gather | solution.py:33
  226.8 7.5 %convolution_bitcast_fusion.2 = f32[8,256,2,512]{1,3,2,0:T(8,128)} fusion(bf16[8,2,256,256]{3,2,1,0:T(8,128)(2,1)S(1)} %gather_fusion, bf16[8,256,512]{2,1,0:T(8,128)(2,1)} %gather_fusion.1, pred[8]{0:T(512)(128)(4,1)S(1)} %get-tuple-element.202, pred[8]{0:T(512)(128)(4,1)S(1)} %get-tuple-element.203, ...), kind=kOutput, calls=%fused_computation.6.clone.1 | convolution fusion | flops 1081081856 | bytes 14680084 | tf_op jit(solution)/shard_map/while/body/eval_jaxpr/tsab,sbm->satm/dot_general | solution.py:34
  247.6 3.3 fusion.59
  252.8 3.3 fusion.60
  268.0 3.3 fusion.63
  273.3 3.4 fusion.64
  279.4 3.5 gather_fusion
  282.9 6.7 %gather_fusion.1 = bf16[8,256,512]{2,1,0:T(8,128)(2,1)} fusion(bf16[48,256,512]{2,1,0:T(8,128)(2,1)} %get-tuple-element.253, s32[1024]{0:T(1024)S(1)} %pad_clamp_fusion.6), kind=kCustom, calls=%fused_computation.clone.1 | custom fusion | bytes 4194336 | tf_op jit(solution)/shard_map/while/body/eval_jaxpr/jit(_take)/gather | solution.py:33
  289.7 7.4 %convolution_bitcast_fusion.2 = f32[8,256,2,512]{1,3,2,0:T(8,128)} fusion(bf16[8,2,256,256]{3,2,1,0:T(8,128)(2,1)S(1)} %gather_fusion, bf16[8,256,512]{2,1,0:T(8,128)(2,1)} %gather_fusion.1, pred[8]{0:T(512)(128)(4,1)S(1)} %get-tuple-element.202, pred[8]{0:T(512)(128)(4,1)S(1)} %get-tuple-element.203, ...), kind=kOutput, calls=%fused_computation.6.clone.1 | convolution fusion | flops 1081081856 | bytes 14680084 | tf_op jit(solution)/shard_map/while/body/eval_jaxpr/tsab,sbm->satm/dot_general | solution.py:34
  310.6 3.3 fusion.59
  320.9 3.3 fusion.61
  331.0 3.3 fusion.63
  336.2 3.3 fusion.64
  342.4 3.5 gather_fusion
  345.8 6.6 %gather_fusion.1 = bf16[8,256,512]{2,1,0:T(8,128)(2,1)} fusion(bf16[48,256,512]{2,1,0:T(8,128)(2,1)} %get-tuple-element.253, s32[1024]{0:T(1024)S(1)} %pad_clamp_fusion.6), kind=kCustom, calls=%fused_computation.clone.1 | custom fusion | bytes 4194336 | tf_op jit(solution)/shard_map/while/body/eval_jaxpr/jit(_take)/gather | solution.py:33
  352.5 7.4 %convolution_bitcast_fusion.2 = f32[8,256,2,512]{1,3,2,0:T(8,128)} fusion(bf16[8,2,256,256]{3,2,1,0:T(8,128)(2,1)S(1)} %gather_fusion, bf16[8,256,512]{2,1,0:T(8,128)(2,1)} %gather_fusion.1, pred[8]{0:T(512)(128)(4,1)S(1)} %get-tuple-element.202, pred[8]{0:T(512)(128)(4,1)S(1)} %get-tuple-element.203, ...), kind=kOutput, calls=%fused_computation.6.clone.1 | convolution fusion | flops 1081081856 | bytes 14680084 | tf_op jit(solution)/shard_map/while/body/eval_jaxpr/tsab,sbm->satm/dot_general | solution.py:34
  373.3 3.3 fusion.59
  378.5 3.3 fusion.60
  383.7 3.3 fusion.61
  388.9 3.3 fusion.62
  399.0 3.3 fusion.64
  402.4 4.0 copy.19
  406.4 10.8 %fusion.32 = f32[2048,2,512]{0,2,1:T(8,128)} fusion(bf16[1536,2,512]{2,0,1:T(8,128)(2,1)S(1)} %bitcast.107, bf16[1536,2048]{1,0:T(8,128)(2,1)} %all-gather.8.cloned.1.call-done), kind=kOutput, calls=%fused_computation.56 | convolution fusion | flops 6442450944 | bytes 17825792 | tf_op jit(solution)/shard_map/kn,ktm->ntm/dot_general | solution.py:49
  417.2 70.9 %reduce-scatter.2.cloned.1.call-done = f32[256,2,512]{0,2,1:T(8,128)} async-done(((f32[2048,2,512]{0,2,1:T(8,128)}), f32[256,2,512]{0,2,1:T(8,128)}) %reduce-scatter.2.cloned.1.call-update) | async-done | bytes 1048592 | tf_op jit(solution)/shard_map/reduce_scatter | solution.py:48
  (64 shorter events, 51.4 us)
Async XLA Ops:
  6.5 68.6 %all-gather.6.cloned.1.call-start = ((), (), s32[]{:S(2)}) async-start(), calls=%async_computation.3 | async-start | bytes 3932160 | tf_op jit(solution)/shard_map/all_gather | solution.py:15
  7.3 202.3 %all-gather.4.cloned.1.call-start = ((), (), s32[]{:S(2)}) async-start(), calls=%async_computation.2 | async-start | bytes 14155776 | tf_op jit(solution)/shard_map/all_gather | solution.py:18
  88.4 115.0 %all-to-all-start = ((bf16[2,24,256,256]{3,2,0,1:T(8,128)(2,1)}), bf16[2,24,256,256]{3,2,0,1:T(8,128)(2,1)}, u32[]{:S(2)}, u32[]{:S(2)}) async-start(bf16[2,24,256,256]{3,2,0,1:T(8,128)(2,1)} %select_bitcast_fusion), calls=%async_computation | async-start | bytes 12582912 | tf_op jit(solution)/shard_map/all_to_all | solution.py:17
  93.2 313.2 %all-gather.8.cloned.1.call-start = ((), (), s32[]{:S(2)}) async-start(), calls=%async_computation.4 | async-start | bytes 7864320 | tf_op jit(solution)/shard_map/all_gather | solution.py:20
  93.9 394.2 %reduce-scatter.2.cloned.1.call-start = ((), (), s32[]{:S(2)}) async-start(), calls=%async_computation.5 | async-start | bytes 9437184 | tf_op jit(solution)/shard_map/reduce_scatter | solution.py:48
  209.5 3.3 copy-start
  209.5 3.3 copy-start.1
  209.5 3.3 copy-start.2
Sparse Core Ops, SparseCore 0:
  8.9 66.1 all-gather.5
  77.0 130.5 all-gather.3
  209.2 115.3 all-gather.7
  417.4 70.7 reduce-scatter.1
where the time goes:
time: 499 us; the launch traced here: 497 us
  waiting for transfers between devices  248 us (50%)
  other arithmetic  86.3 us (17%)
  local copies, waits for them, and re-layouts  60.6 us (12%)
  loops' own time  50.2 us (10%)
  matrix products  33.2 us (7%)
  between operations  13.8 us (3%)
    all_to_all x1, waiting for transfers between devices, shards(): lax.all_to_all(packed, 'blk', split_axis=1, concat_axis=1, tiled=True)  109 us
    dynamic_update_slice x24, other arithmetic, accumulate(): totals = lax.dynamic_update_slice_in_dim(totals, updated, target, 0)  78.8 us
    reduce_scatter x1, waiting for transfers between devices, shards(): lax.psum_scatter(jnp.einsum('kn,ktm->ntm', own_rows, folded, preferred_el...  70.9 us
    all_gather x1, waiting for transfers between devices, shards(): screen_whole = lax.all_gather(screen_tiles, 'orb', axis=2, tiled=True)  66.2 us
    another operation x1, loops' own time, shards(): totals, unused = lax.scan(accumulate, empty, starts)  50.2 us
    dot_general x3, matrix products, accumulate(): jnp.einsum('tsab,sbm->satm', sigma, blocks, preferred_element_type=jnp.fl...  22.3 us
    gather x3, local copies, waits for them, and re-layouts, accumulate(): blocks = jnp.take(panel_blocks, columns, axis=0)  20.2 us
    gather x3, local copies, waits for them, and re-layouts, accumulate(): screen_part = jnp.take(arrived, which, axis=1)  11.1 us
  transfers between devices with their start and end apart: 5, of which 3 were waited for; matrix products, arithmetic and copies ran while one was open for 34% of the time, Pallas kernels for 0%

commit v1 on v0

--- a/solution.py
+++ b/solution.py
@@ -2,6 +2,22 @@
 import jax.numpy as jnp
 from jax import lax
 from jax.sharding import PartitionSpec as P
+
+
+def gather_around(x, axis, dim):
+    ways, here, step = (lax.axis_size(axis), lax.axis_index(axis), x.shape[dim])
+    shape = [n * ways if d == dim else n for d, n in enumerate(x.shape)]
+    full = lax.dynamic_update_slice_in_dim(jnp.zeros(shape, x.dtype), x, here * step, axis=dim)
+    going_up = going_down = x
+    for far in range(1, ways // 2 + 1):
+        going_up = lax.ppermute(going_up, axis, [(d, (d + 1) % ways) for d in range(ways)])
+        full = lax.dynamic_update_slice_in_dim(full, going_up, (here - far) % ways * step, axis=dim)
+        if 2 * far < ways:
+            going_down = lax.ppermute(going_down, axis, [(d, (d - 1) % ways) for d in range(ways)])
+            full = lax.dynamic_update_slice_in_dim(
+                full, going_down, (here + far) % ways * step, axis=dim
+            )
+    return full
 
 
 def shards(
@@ -12,7 +28,7 @@
     owned_blocks = coeffs.shape[0] // width
     orbital_local = coeffs.shape[1]
     outgoing = send_slot.reshape(-1)
-    screen_whole = lax.all_gather(screen_tiles, "orb", axis=2, tiled=True)
+    screen_whole = gather_around(screen_tiles, "orb", 2)
     packed = jnp.take(screen_whole, outgoing, axis=1)
     arrived = lax.all_to_all(packed, "blk", split_axis=1, concat_axis=1, tiled=True)
     panel = lax.all_gather(coeffs, "blk", axis=0, tiled=True)

time: 499 us -> 445 us (0.89)
  waiting for transfers between devices: 248 us -> 187 us
  starting transfers between devices: 4.94 us -> 10.1 us
    all_gather x1 -> x0, waiting for transfers between devices: 66.2 us -> none  [shards(): screen_whole = lax.all_gather(screen_tiles, 'orb', axis=2, tiled=True)]
    ppermute x0 -> x3, waiting for transfers between devices: none -> 46.4 us  [the longest x2 33.6 us: gather_around(): lax.ppermute(going_up, axis, [(d, (d + 1) % ways) for d in range(ways)])]
    all_to_all x1, waiting for transfers between devices: 109 us -> 70.1 us  [shards(): lax.all_to_all(packed, 'blk', split_axis=1, concat_axis=1, tiled=True)]
    ppermute x0 -> x3, starting transfers between devices: none -> 5.17 us  [the longest x2 3.08 us: gather_around(): lax.ppermute(going_up, axis, [(d, (d + 1) % ways) for d in range(ways)])]
  transfers between devices with their start and end apart: 5 -> 7, of which waited for: 3 -> 5; matrix products, arithmetic and copies ran while one was open for 34% -> 38% of each run, Pallas kernels for 0% -> 0%
where the time goes in v1:
time: 445 us; the launch traced here: 443 us
  waiting for transfers between devices  187 us (42%)
  other arithmetic  85.4 us (19%)
  local copies, waits for them, and re-layouts  63 us (14%)
  loops' own time  50.2 us (11%)
  matrix products  33.1 us (7%)
  between operations  13.8 us (3%)
  starting transfers between devices  10.1 us (2%)
    dynamic_update_slice x24, other arithmetic, accumulate(): totals = lax.dynamic_update_slice_in_dim(totals, updated, target, 0)  78.7 us
    all_to_all x1, waiting for transfers between devices, shards(): lax.all_to_all(packed, 'blk', split_axis=1, concat_axis=1, tiled=True)  70.1 us
    reduce_scatter x1, waiting for transfers between devices, shards(): lax.psum_scatter(jnp.einsum('kn,ktm->ntm', own_rows, folded, preferred_el...  69.3 us
    another operation x1, loops' own time, shards(): totals, unused = lax.scan(accumulate, empty, starts)  50.2 us
    ppermute x2, waiting for transfers between devices, gather_around(): lax.ppermute(going_up, axis, [(d, (d + 1) % ways) for d in range(ways)])  33.6 us
    dot_general x3, matrix products, accumulate(): jnp.einsum('tsab,sbm->satm', sigma, blocks, preferred_element_type=jnp.fl...  22.3 us
    gather x3, local copies, waits for them, and re-layouts, accumulate(): blocks = jnp.take(panel_blocks, columns, axis=0)  19.9 us
    ppermute x1, waiting for transfers between devices, gather_around(): lax.ppermute(going_down, axis, [(d, (d - 1) % ways) for d in range(ways)])  12.8 us
  transfers between devices with their start and end apart: 7, of which 5 were waited for; matrix products, arithmetic and copies ran while one was open for 38% of the time, Pallas kernels for 0%

profile of v1, /device:TPU:0, one launch (start us, length us, event | category | flops | bytes accessed | tf_op | source)
XLA Modules:
  0.0 442.9 jit_solution(3038393809071013155)
XLA Ops:
  13.3 17.8 %collective-permute-done = bf16[2,12,64,256]{3,2,1,0:T(8,128)(2,1)} collective-permute-done((bf16[2,12,64,256]{3,2,1,0:T(8,128)(2,1)}, bf16[2,12,64,256]{3,2,1,0:T(8,128)(2,1)}, u32[]{:S(2)}, u32[]{:S(2)}) %collective-permute-start) | collective-permute-done | bytes 786464 | tf_op jit(solution)/shard_map/ppermute | solution.py:13
  33.9 12.8 %collective-permute-done.1 = bf16[2,12,64,256]{3,2,1,0:T(8,128)(2,1)} collective-permute-done((bf16[2,12,64,256]{3,2,1,0:T(8,128)(2,1)}, bf16[2,12,64,256]{3,2,1,0:T(8,128)(2,1)}, u32[]{:S(2)}, u32[]{:S(2)}) %collective-permute-start.1) | collective-permute-done | bytes 786464 | tf_op jit(solution)/shard_map/ppermute | solution.py:16
  48.1 15.8 %collective-permute-done.2 = bf16[2,12,64,256]{3,2,1,0:T(8,128)(2,1)} collective-permute-done((bf16[2,12,64,256]{3,2,1,0:T(8,128)(2,1)}, bf16[2,12,64,256]{3,2,1,0:T(8,128)(2,1)}, u32[]{:S(2)}, u32[]{:S(2)}) %collective-permute-start.2) | collective-permute-done | bytes 786464 | tf_op jit(solution)/shard_map/ppermute | solution.py:13
  65.2 4.4 gather_fusion.2
  69.6 6.1 %select_bitcast_fusion = bf16[2,24,256,256]{3,2,0,1:T(8,128)(2,1)} fusion(bf16[24,2,256,256]{3,2,1,0:T(8,128)(2,1)} %gather_fusion.2, pred[24]{0:T(512)(128)(4,1)S(1)} %compare_and_fusion.2), kind=kLoop, calls=%fused_computation.55 | loop fusion | flops 3145728 | bytes 12582936 | tf_op jit(solution)/shard_map/jit(_take)/select_n | solution.py:32
  75.7 4.8 %all-to-all-start = ((bf16[2,24,256,256]{3,2,0,1:T(8,128)(2,1)}), bf16[2,24,256,256]{3,2,0,1:T(8,128)(2,1)}, u32[]{:S(2)}, u32[]{:S(2)}) async-start(bf16[2,24,256,256]{3,2,0,1:T(8,128)(2,1)} %select_bitcast_fusion), calls=%async_computation | async-start | bytes 12582912 | tf_op jit(solution)/shard_map/all_to_all | solution.py:33
  82.0 70.1 %all-to-all-done = bf16[2,24,256,256]{3,2,0,1:T(8,128)(2,1)} async-done(((bf16[2,24,256,256]{3,2,0,1:T(8,128)(2,1)}), bf16[2,24,256,256]{3,2,0,1:T(8,128)(2,1)}, u32[]{:S(2)}, u32[]{:S(2)}) %all-to-all-start) | async-done | bytes 6291488 | tf_op jit(solution)/shard_map/all_to_all | solution.py:33
  152.1 6.2 %copy.18 = bf16[2,24,256,256]{3,2,1,0:T(8,128)(2,1)} copy(bf16[2,24,256,256]{3,2,0,1:T(8,128)(2,1)} %all-to-all-done) | data formatting | bytes 12582912 | tf_op jit(solution)/shard_map/while | solution.py:62
  161.5 188.4 %while.10 = (s32[]{:T(128)}, f32[6,256,2,512]{1,3,2,0:T(8,128)}, s32[3]{0:T(128)S(1)}, s32[24]{0:T(128)S(1)}, f32[24]{0:T(128)S(1)}, /*index=5*/s32[1,24]{1,0:T(...) while((s32[]{:T(128)}, f32[6,256,2,512]{1,3,2,0:T(8,128)}, ...), condition=%wide.region_1.2_spmd, body=%wide.region_0.1_spmd.sunk | while | flops 1085278336 | bytes 48247880 | solution.py:62
  164.4 3.5 gather_fusion
  167.9 6.7 %gather_fusion.1 = bf16[8,256,512]{2,1,0:T(8,128)(2,1)} fusion(bf16[48,256,512]{2,1,0:T(8,128)(2,1)} %get-tuple-element.253, s32[1024]{0:T(1024)S(1)} %pad_clamp_fusion.6), kind=kCustom, calls=%fused_computation.clone.1 | custom fusion | bytes 4194336 | tf_op jit(solution)/shard_map/while/body/eval_jaxpr/jit(_take)/gather | solution.py:49
  174.6 7.4 %convolution_bitcast_fusion.2 = f32[8,256,2,512]{1,3,2,0:T(8,128)} fusion(bf16[8,2,256,256]{3,2,1,0:T(8,128)(2,1)S(1)} %gather_fusion, bf16[8,256,512]{2,1,0:T(8,128)(2,1)} %gather_fusion.1, pred[8]{0:T(512)(128)(4,1)S(1)} %get-tuple-element.202, pred[8]{0:T(512)(128)(4,1)S(1)} %get-tuple-element.203, ...), kind=kOutput, calls=%fused_computation.6.clone.1 | convolution fusion | flops 1081081856 | bytes 14680084 | tf_op jit(solution)/shard_map/while/body/eval_jaxpr/tsab,sbm->satm/dot_general | solution.py:50
  195.4 3.3 fusion.59
  200.6 3.3 fusion.60
  215.8 3.3 fusion.63
  221.0 3.3 fusion.64
  227.2 3.5 gather_fusion
  230.7 6.6 %gather_fusion.1 = bf16[8,256,512]{2,1,0:T(8,128)(2,1)} fusion(bf16[48,256,512]{2,1,0:T(8,128)(2,1)} %get-tuple-element.253, s32[1024]{0:T(1024)S(1)} %pad_clamp_fusion.6), kind=kCustom, calls=%fused_computation.clone.1 | custom fusion | bytes 4194336 | tf_op jit(solution)/shard_map/while/body/eval_jaxpr/jit(_take)/gather | solution.py:49
  237.3 7.4 %convolution_bitcast_fusion.2 = f32[8,256,2,512]{1,3,2,0:T(8,128)} fusion(bf16[8,2,256,256]{3,2,1,0:T(8,128)(2,1)S(1)} %gather_fusion, bf16[8,256,512]{2,1,0:T(8,128)(2,1)} %gather_fusion.1, pred[8]{0:T(512)(128)(4,1)S(1)} %get-tuple-element.202, pred[8]{0:T(512)(128)(4,1)S(1)} %get-tuple-element.203, ...), kind=kOutput, calls=%fused_computation.6.clone.1 | convolution fusion | flops 1081081856 | bytes 14680084 | tf_op jit(solution)/shard_map/while/body/eval_jaxpr/tsab,sbm->satm/dot_general | solution.py:50
  258.2 3.3 fusion.59
  278.6 3.3 fusion.63
  283.8 3.3 fusion.64
  290.0 3.5 gather_fusion
  293.5 6.6 %gather_fusion.1 = bf16[8,256,512]{2,1,0:T(8,128)(2,1)} fusion(bf16[48,256,512]{2,1,0:T(8,128)(2,1)} %get-tuple-element.253, s32[1024]{0:T(1024)S(1)} %pad_clamp_fusion.6), kind=kCustom, calls=%fused_computation.clone.1 | custom fusion | bytes 4194336 | tf_op jit(solution)/shard_map/while/body/eval_jaxpr/jit(_take)/gather | solution.py:49
  300.1 7.4 %convolution_bitcast_fusion.2 = f32[8,256,2,512]{1,3,2,0:T(8,128)} fusion(bf16[8,2,256,256]{3,2,1,0:T(8,128)(2,1)S(1)} %gather_fusion, bf16[8,256,512]{2,1,0:T(8,128)(2,1)} %gather_fusion.1, pred[8]{0:T(512)(128)(4,1)S(1)} %get-tuple-element.202, pred[8]{0:T(512)(128)(4,1)S(1)} %get-tuple-element.203, ...), kind=kOutput, calls=%fused_computation.6.clone.1 | convolution fusion | flops 1081081856 | bytes 14680084 | tf_op jit(solution)/shard_map/while/body/eval_jaxpr/tsab,sbm->satm/dot_general | solution.py:50
  320.9 3.3 fusion.59
  326.1 3.3 fusion.60
  331.3 3.3 fusion.61
  346.6 3.3 fusion.64
  350.0 4.0 copy.19
  354.0 10.8 %fusion.32 = f32[2048,2,512]{0,2,1:T(8,128)} fusion(bf16[1536,2,512]{2,0,1:T(8,128)(2,1)S(1)} %bitcast.107, bf16[1536,2048]{1,0:T(8,128)(2,1)} %all-gather.5.cloned.1.call-done), kind=kOutput, calls=%fused_computation.56 | convolution fusion | flops 6442450944 | bytes 17825792 | tf_op jit(solution)/shard_map/kn,ktm->ntm/dot_general | solution.py:65
  364.8 69.3 %reduce-scatter.2.cloned.1.call-done = f32[256,2,512]{0,2,1:T(8,128)} async-done(((f32[2048,2,512]{0,2,1:T(8,128)}), f32[256,2,512]{0,2,1:T(8,128)}) %reduce-scatter.2.cloned.1.call-update) | async-done | bytes 1048592 | tf_op jit(solution)/shard_map/reduce_scatter | solution.py:64
  (72 shorter events, 67.7 us)
Async XLA Ops:
  6.5 151.8 %all-gather.3.cloned.1.call-start = ((), (), s32[]{:S(2)}) async-start(), calls=%async_computation.2 | async-start | bytes 14155776 | tf_op jit(solution)/shard_map/all_gather | solution.py:34
  7.3 23.8 %collective-permute-start = (bf16[2,12,64,256]{3,2,1,0:T(8,128)(2,1)}, bf16[2,12,64,256]{3,2,1,0:T(8,128)(2,1)}, u32[]{:S(2)}, u32[]{:S(2)}) collective-permute-start(bf16[2,12,64,256]{3,2,1,0:T(8,128)(2,1)} %param.11), channel_id=1, source_target_pairs={{0,1},{1,2},{2,3},{3,0},{4,5},{5,6},{6,7},{7,4},{8,9},{9,10},{10,1... | collective-permute-start | bytes 2359304 | tf_op jit(solution)/shard_map/ppermute | solution.py:13
  10.3 36.4 %collective-permute-start.1 = (bf16[2,12,64,256]{3,2,1,0:T(8,128)(2,1)}, bf16[2,12,64,256]{3,2,1,0:T(8,128)(2,1)}, u32[]{:S(2)}, u32[]{:S(2)}) collective-permute-start(bf16[2,12,64,256]{3,2,1,0:T(8,128)(2,1)} %param.11), channel_id=1, source_target_pairs={{0,3},{1,0},{2,1},{3,2},{4,7},{5,4},{6,5},{7,6},{8,11},{9,8},{10,9... | collective-permute-start | bytes 2359304 | tf_op jit(solution)/shard_map/ppermute | solution.py:16
  31.1 32.9 %collective-permute-start.2 = (bf16[2,12,64,256]{3,2,1,0:T(8,128)(2,1)}, bf16[2,12,64,256]{3,2,1,0:T(8,128)(2,1)}, u32[]{:S(2)}, u32[]{:S(2)}) collective-permute-start(bf16[2,12,64,256]{3,2,1,0:T(8,128)(2,1)} %collective-permute-done), channel_id=1, source_target_pairs={{0,1},{1,2},{2,3},{3,0},{4,5},{5,6},{6,7},{7,4},{8,9},{9,10},{10,1... | collective-permute-start | bytes 2359304 | tf_op jit(solution)/shard_map/ppermute | solution.py:13
  75.7 76.4 %all-to-all-start = ((bf16[2,24,256,256]{3,2,0,1:T(8,128)(2,1)}), bf16[2,24,256,256]{3,2,0,1:T(8,128)(2,1)}, u32[]{:S(2)}, u32[]{:S(2)}) async-start(bf16[2,24,256,256]{3,2,0,1:T(8,128)(2,1)} %select_bitcast_fusion), calls=%async_computation | async-start | bytes 12582912 | tf_op jit(solution)/shard_map/all_to_all | solution.py:33
  80.5 273.5 %all-gather.5.cloned.1.call-start = ((), (), s32[]{:S(2)}) async-start(), calls=%async_computation.3 | async-start | bytes 7864320 | tf_op jit(solution)/shard_map/all_gather | solution.py:36
  81.3 352.9 %reduce-scatter.2.cloned.1.call-start = ((), (), s32[]{:S(2)}) async-start(), calls=%async_computation.4 | async-start | bytes 9437184 | tf_op jit(solution)/shard_map/reduce_scatter | solution.py:64
  158.3 3.3 copy-start
  158.3 3.3 copy-start.1
  158.3 3.3 copy-start.2
Sparse Core Ops, SparseCore 0:
  9.2 74.8 all-gather.2
  85.7 115.3 all-gather.4
  365.0 69.1 reduce-scatter.1
